TPU v7x, 512 devices: a whole 4x4x16 slice. The times are simulated.
512 devices in a mesh: gx: 32 (over z, core), gy: 16 (over y, x).
Axes of the slice: x: 4, y: 4, z: 16, core: 2. Of those that a mesh axis runs over, the one named last changes fastest.
Arguments:
- residual: float32 [3, 512, 256, 128], P(None, 'gx', 'gy'), may hold values from -6 to 6
- stiffness: float32 [512, 256], P('gx', 'gy'), may hold values from 0.5 to 2
- local_inverse: bfloat16 [32, 16, 1024, 1024], P('gx', 'gy'), as said below
- coarse_basis: bfloat16 [32, 16, 8, 1024], P('gx', 'gy'), may hold values from -0.5 to 0.5
- coarse_rows: bfloat16 [32, 16, 8, 4096], P('gx', 'gy'), as said below
- send_rows: int32 [32, 16, 4, 64], P('gx', 'gy'), may hold values from 0 to 767, as said below
- partition_map: int32 [512], replicated, may hold values from 0 to 511, as said below
Outputs:
- solution: float32 [3, 512, 256, 128], P(None, 'gx', 'gy')
- final: float32 [3, 512, 256, 128], P(None, 'gx', 'gy')
Inputs may be any that keep to these rules, and one draw needn't show every extreme that they name: `send_rows`: for each subdomain, the lists j = 0, 1 (lower and upper neighbour along gx) and j = 2, 3 (lower and upper neighbour along gy) each name 64 distinct owned rows, all of them in the two layers of cells nearest that neighbour. `partition_map`: A permutation of the device numbers. `coarse_rows`: with its columns put in device order through partition_map, the 4096-square matrix S is symmetric. `local_inverse`: each subdomain's block is symmetric.
All inputs are finite; a program needn't handle non-finite values.
Results may differ from a plain program's by a relative error of at most 0.0057.
Values may be sent and summed in bfloat16 or wider, within the bound.
No kernel may reach another device: no remote copies, remote signals or barrier semaphores. Data moves between devices by JAX's collectives and lax.ppermute only.
A program may use at most 64 MiB of HBM per device.

v0:
```python
import jax
import jax.numpy as jnp
from jax import lax
from jax.sharding import PartitionSpec as P


def with_halo(block, sides, width):
    for axis, dim in sides:
        count = lax.axis_size(axis)
        forward = [(i, i + 1) for i in range(count - 1)]
        backward = [(target, source) for source, target in forward]
        low = lax.ppermute(
            lax.slice_in_dim(block, block.shape[dim] - width, None, axis=dim), axis, forward
        )
        high = lax.ppermute(lax.slice_in_dim(block, 0, width, axis=dim), axis, backward)
        block = jnp.concatenate([low, block, high], axis=dim)
    return block


def trade_along_gx(pair):
    return with_halo(pair, (("gx", 0),), 1)


def trade_along_gy(pair):
    return with_halo(pair, (("gy", 0),), 1)


def operate(values, stiffness):
    padded = with_halo(values, (("gx", 1), ("gy", 2)), 1)
    beside = padded[:, 2:, 1:-1] + padded[:, :-2, 1:-1] + padded[:, 1:-1, 2:] + padded[:, 1:-1, :-2]
    return (4.0 + stiffness[None, :, :, None]) * values - beside


def coarse_solve(coarse_in, ordered):
    return jnp.dot(
        ordered,
        lax.all_gather(coarse_in, ("gx", "gy"), axis=0, tiled=True),
        preferred_element_type=jnp.float32,
    )


def precondition(values, inverse, basis_rows, row_lists, ordered):
    own_rows = values.reshape(-1, values.shape[-1])
    own_count = own_rows.shape[0]
    margin = row_lists.shape[1]
    outgoing = jnp.take(own_rows, row_lists, axis=0)
    from_gx = trade_along_gx(outgoing[0:2])
    from_gy = trade_along_gy(outgoing[2:4])
    subdomain = jnp.concatenate([own_rows, from_gx[0], from_gx[3], from_gy[0], from_gy[3]], axis=0)
    subdomain = subdomain.astype(jnp.bfloat16)
    coarse_in = jnp.dot(basis_rows, subdomain, preferred_element_type=jnp.float32).astype(
        jnp.bfloat16
    )
    coarse_out = coarse_solve(coarse_in, ordered).astype(jnp.bfloat16)
    patch = jnp.dot(inverse, subdomain, preferred_element_type=jnp.float32)
    patch = patch + lax.dot_general(
        basis_rows, coarse_out, (((0,), (0,)), ((), ())), preferred_element_type=jnp.float32
    )
    back_gx = trade_along_gx(
        jnp.stack(
            [
                patch[own_count : own_count + margin],
                patch[own_count + margin : own_count + 2 * margin],
            ]
        )
    )
    back_gy = trade_along_gy(
        jnp.stack(
            [
                patch[own_count + 2 * margin : own_count + 3 * margin],
                patch[own_count + 3 * margin :],
            ]
        )
    )
    update = patch[:own_count]
    update = update.at[row_lists[0]].add(back_gx[0])
    update = update.at[row_lists[1]].add(back_gx[3])
    update = update.at[row_lists[2]].add(back_gy[0])
    update = update.at[row_lists[3]].add(back_gy[3])
    return update.reshape(values.shape)


def per_device(
    residual, stiffness, local_inverse, coarse_basis, coarse_rows, send_rows, partition_map
):
    inverse = local_inverse[0, 0]
    basis_rows = coarse_basis[0, 0]
    row_lists = send_rows[0, 0]
    device_count = partition_map.shape[0]
    coarse_width = basis_rows.shape[0]
    stored = coarse_rows[0, 0].reshape(coarse_width, device_count, coarse_width)
    ordered = jnp.take(stored, partition_map, axis=1).reshape(
        coarse_width, device_count * coarse_width
    )
    first_pass = precondition(residual, inverse, basis_rows, row_lists, ordered)
    middle = residual - operate(first_pass, stiffness)
    second_pass = precondition(middle, inverse, basis_rows, row_lists, ordered)
    solution = first_pass + second_pass
    return (solution, residual - operate(solution, stiffness))


def solution(mesh):
    placed = (
        P(None, "gx", "gy", None),
        P("gx", "gy"),
        P("gx", "gy", None, None),
        P("gx", "gy", None, None),
        P("gx", "gy", None, None),
        P("gx", "gy", None, None),
        P(),
    )
    return jax.shard_map(
        per_device,
        mesh=mesh,
        in_specs=placed,
        out_specs=(P(None, "gx", "gy", None), P(None, "gx", "gy", None)),
        check_vma=False,
    )
```

profile of v0, /device:TPU:40, one launch (start us, length us, event | category | flops | bytes accessed | tf_op | source)
XLA Modules:
  0.0 486.4 jit_solution(15836216177516421753)
XLA Ops:
  9.5 1.7 gather_fusion.1
  11.4 1.9 collective-permute-start
  13.3 3.6 collective-permute-start.1
  16.9 3.4 collective-permute-start.2
  20.4 4.6 collective-permute-start.3
  26.4 1.4 fusion.18
  27.9 3.0 reshape_squeeze.3
  30.9 1.9 copy.29
  32.8 2.4 gather_fusion
  35.2 1.4 copy.30
  36.6 1.5 gather.10
  38.4 163.3 %all-gather.3.cloned.1.call-done = bf16[4096,128]{1,0:T(8,128)(2,1)} async-done(((bf16[8,128]{1,0:T(8,128)(2,1)}), bf16[4096,128]{1,0:T(8,128)(2,1)}) %all-gather.3.cloned.1.call-update) | async-done | bytes 1048592 | tf_op jit(solution)/shard_map/all_gather | solution.py:37
  201.7 1.7 fusion.16
  205.0 2.1 collective-permute-start.4
  207.2 3.4 collective-permute-start.5
  210.6 3.3 collective-permute-start.6
  213.9 4.7 collective-permute-start.7
  220.8 1.2 scatter_fusion
  222.1 1.2 scatter_fusion.1
  223.3 1.2 scatter_fusion.2
  224.5 1.2 scatter_fusion.3
  225.7 1.9 collective-permute-start.8
  227.6 2.4 collective-permute-start.9
  230.1 2.7 collective-permute-done.9
  232.8 6.3 %collective-permute-start.10 = (f32[3,18,1,128]{3,2,1,0:T(1,128)S(1)}, f32[3,18,1,128]{3,2,1,0:T(1,128)S(1)}, u32[]{:S(2)}, u32[]{:S(2)}) collective-permute-start(f32[3,18,1,128]{3,2,1,0:T(1,128)S(1)} %get-tuple-element.13), channel_id=1, source_target_pairs={{1,0},{2,1},{3,2},{4,3},{5,4},{6,5},{7,6},{8,7},{9,8},{10,9},{11,1... | collective-permute-start | bytes 82952 | tf_op jit(solution)/shard_map/ppermute | solution.py:15
  239.1 1.9 collective-permute-start.11
  241.1 5.9 %collective-permute-done.11 = f32[3,18,1,128]{3,2,1,0:T(1,128)S(1)} collective-permute-done((f32[3,18,1,128]{3,2,1,0:T(1,128)S(1)}, f32[3,18,1,128]{3,2,1,0:T(1,128)S(1)}, u32[]{:S(2)}, u32[]{:S(2)}) %collective-permute-start.11) | collective-permute-done | bytes 27680 | tf_op jit(solution)/shard_map/ppermute | solution.py:12
  248.2 1.9 collective-permute-start.12
  250.1 3.6 collective-permute-start.13
  253.8 1.9 collective-permute-start.14
  255.7 6.0 %collective-permute-start.15 = (bf16[1,64,128]{2,1,0:T(8,128)(2,1)S(1)}, bf16[1,64,128]{2,1,0:T(8,128)(2,1)S(1)}, u32[]{:S(2)}, u32[]{:S(2)}) collective-permute-start(bf16[1,64,128]{2,1,0:T(8,128)(2,1)S(1)} %get-tuple-element.19), channel_id=1, source_target_pairs={{1,0},{2,1},{3,2},{4,3},{5,4},{6,5},{7,6},{8,7},{9,8},{10,9},{11,1... | collective-permute-start | bytes 49160 | tf_op jit(solution)/shard_map/ppermute | solution.py:15
  261.8 1.4 collective-permute-done.15
  264.6 168.2 %all-gather.5.cloned.1.call-done = bf16[4096,128]{1,0:T(8,128)(2,1)} async-done(((bf16[8,128]{1,0:T(8,128)(2,1)}), bf16[4096,128]{1,0:T(8,128)(2,1)}) %all-gather.5.cloned.1.call-update) | async-done | bytes 1048592 | tf_op jit(solution)/shard_map/all_gather | solution.py:37
  432.8 1.7 fusion.17
  434.5 1.8 fusion.13
  437.1 2.1 collective-permute-start.16
  439.3 3.4 collective-permute-start.17
  442.7 3.3 collective-permute-start.18
  446.0 4.7 collective-permute-start.19
  451.4 1.1 copy.36
  456.7 1.1 scatter_fusion.4
  457.8 1.1 scatter_fusion.5
  461.2 1.9 collective-permute-start.20
  463.1 2.4 collective-permute-start.21
  465.5 2.7 collective-permute-done.21
  468.3 2.5 collective-permute-start.22
  470.8 3.4 collective-permute-start.23
  474.2 4.5 collective-permute-done.23
  (112 shorter events, 19.6 us)
Async XLA Ops:
  7.2 196.3 %copy-start = (bf16[1,1,1024,1024]{3,2,1,0:T(8,128)(2,1)S(1)}, bf16[1,1,1024,1024]{3,2,1,0:T(8,128)(2,1)}, u32[]{:S(2)}) copy-start(bf16[1,1,1024,1024]{3,2,1,0:T(8,128)(2,1)} %param.11) | copy-start | bytes 6291460
  7.2 194.5 %all-gather.3.cloned.1.call-start = ((), (), s32[]{:S(2)}) async-start(), calls=%async_computation | async-start | bytes 1050624 | tf_op jit(solution)/shard_map/all_gather | solution.py:37
  8.7 11.6 %copy-start.14 = (pred[4,64]{1,0:T(4,128)(4,1)}, pred[4,64]{1,0:T(4,128)(4,1)S(1)}, u32[]{:S(2)}) copy-start(pred[4,64]{1,0:T(4,128)(4,1)S(1)} %compare_and_fusion) | copy-start | bytes 772
  9.5 10.8 %copy-start.10 = (s32[1024]{0:T(1024)}, s32[1024]{0:T(1024)S(1)}, u32[]{:S(2)}) copy-start(s32[1024]{0:T(1024)S(1)} %get-tuple-element.32) | copy-start | bytes 12292
  11.4 14.6 %collective-permute-start = (bf16[1,64,128]{2,1,0:T(8,128)(2,1)S(1)}, bf16[1,64,128]{2,1,0:T(8,128)(2,1)S(1)}, u32[]{:S(2)}, u32[]{:S(2)}) collective-permute-start(bf16[1,64,128]{2,1,0:T(8,128)(2,1)S(1)} %get-tuple-element.26), channel_id=1, source_target_pairs={{0,16},{16,32},{32,48},{48,64},{64,80},{80,96},{96,112},{112,128},... | collective-permute-start | bytes 49160 | tf_op jit(solution)/shard_map/ppermute | solution.py:12
  13.3 12.7 %collective-permute-start.1 = (bf16[1,64,128]{2,1,0:T(8,128)(2,1)S(1)}, bf16[1,64,128]{2,1,0:T(8,128)(2,1)S(1)}, u32[]{:S(2)}, u32[]{:S(2)}) collective-permute-start(bf16[1,64,128]{2,1,0:T(8,128)(2,1)S(1)} %get-tuple-element.25), channel_id=1, source_target_pairs={{16,0},{32,16},{48,32},{64,48},{80,64},{96,80},{112,96},{128,112},... | collective-permute-start | bytes 49160 | tf_op jit(solution)/shard_map/ppermute | solution.py:15
  16.9 9.1 %collective-permute-start.2 = (bf16[1,64,128]{2,1,0:T(8,128)(2,1)S(1)}, bf16[1,64,128]{2,1,0:T(8,128)(2,1)S(1)}, u32[]{:S(2)}, u32[]{:S(2)}) collective-permute-start(bf16[1,64,128]{2,1,0:T(8,128)(2,1)S(1)} %get-tuple-element.24), channel_id=1, source_target_pairs={{0,1},{1,2},{2,3},{3,4},{4,5},{5,6},{6,7},{7,8},{8,9},{9,10},{10,1... | collective-permute-start | bytes 49160 | tf_op jit(solution)/shard_map/ppermute | solution.py:12
  20.4 6.0 %collective-permute-start.3 = (bf16[1,64,128]{2,1,0:T(8,128)(2,1)S(1)}, bf16[1,64,128]{2,1,0:T(8,128)(2,1)S(1)}, u32[]{:S(2)}, u32[]{:S(2)}) collective-permute-start(bf16[1,64,128]{2,1,0:T(8,128)(2,1)S(1)} %get-tuple-element.23), channel_id=1, source_target_pairs={{1,0},{2,1},{3,2},{4,3},{5,4},{6,5},{7,6},{8,7},{9,8},{10,9},{11,1... | collective-permute-start | bytes 49160 | tf_op jit(solution)/shard_map/ppermute | solution.py:15
  27.8 405.0 %all-gather.5.cloned.1.call-start = ((), (), s32[]{:S(2)}) async-start(), calls=%async_computation.1 | async-start | bytes 1050624 | tf_op jit(solution)/shard_map/all_gather | solution.py:37
  35.2 2.9 copy-start.12
  35.2 166.5 %copy-start.4 = (bf16[1,1,8,1024]{3,2,1,0:T(8,128)(2,1)S(1)}, bf16[1,1,8,1024]{3,2,1,0:T(8,128)(2,1)}, u32[]{:S(2)}) copy-start(bf16[1,1,8,1024]{3,2,1,0:T(8,128)(2,1)} %param.12) | copy-start | bytes 49156
  38.4 165.9 %copy-start.7 = (pred[4096]{0:T(1024)(128)(4,1)}, pred[4096]{0:T(1024)(128)(4,1)S(1)}, u32[]{:S(2)}) copy-start(pred[4096]{0:T(1024)(128)(4,1)S(1)} %broadcast_in_dim.36) | copy-start | bytes 12292
  203.4 15.1 %copy-start.9 = (s32[1,1,4,64]{3,2,1,0:T(4,128)S(1)}, s32[1,1,4,64]{3,2,1,0:T(4,128)}, u32[]{:S(2)}) copy-start(s32[1,1,4,64]{3,2,1,0:T(4,128)} %param.14) | copy-start | bytes 3076
  205.0 14.4 %collective-permute-start.4 = (f32[1,64,128]{1,2,0:T(8,128)}, f32[1,64,128]{1,2,0:T(8,128)}, u32[]{:S(2)}, u32[]{:S(2)}) collective-permute-start(f32[1,64,128]{1,2,0:T(8,128)} %get-tuple-element.10), channel_id=1, source_target_pairs={{0,16},{16,32},{32,48},{48,64},{64,80},{80,96},{96,112},{112,128},... | collective-permute-start | bytes 98312 | tf_op jit(solution)/shard_map/ppermute | solution.py:12
  207.2 13.1 %collective-permute-start.5 = (f32[1,64,128]{1,2,0:T(8,128)}, f32[1,64,128]{1,2,0:T(8,128)S(1)}, u32[]{:S(2)}, u32[]{:S(2)}) collective-permute-start(f32[1,64,128]{1,2,0:T(8,128)} %get-tuple-element.9), channel_id=1, source_target_pairs={{16,0},{32,16},{48,32},{64,48},{80,64},{96,80},{112,96},{128,112},... | collective-permute-start | bytes 98312 | tf_op jit(solution)/shard_map/ppermute | solution.py:15
  210.6 9.8 %collective-permute-start.6 = (f32[1,64,128]{1,2,0:T(8,128)}, f32[1,64,128]{1,2,0:T(8,128)S(1)}, u32[]{:S(2)}, u32[]{:S(2)}) collective-permute-start(f32[1,64,128]{1,2,0:T(8,128)} %get-tuple-element.8), channel_id=1, source_target_pairs={{0,1},{1,2},{2,3},{3,4},{4,5},{5,6},{6,7},{7,8},{8,9},{9,10},{10,1... | collective-permute-start | bytes 98312 | tf_op jit(solution)/shard_map/ppermute | solution.py:12
  213.9 6.9 %collective-permute-start.7 = (f32[1,64,128]{1,2,0:T(8,128)}, f32[1,64,128]{1,2,0:T(8,128)S(1)}, u32[]{:S(2)}, u32[]{:S(2)}) collective-permute-start(f32[1,64,128]{1,2,0:T(8,128)} %get-tuple-element.7), channel_id=1, source_target_pairs={{1,0},{2,1},{3,2},{4,3},{5,4},{6,5},{7,6},{8,7},{9,8},{10,9},{11,1... | collective-permute-start | bytes 98312 | tf_op jit(solution)/shard_map/ppermute | solution.py:15
  219.2 27.8 %copy-start.1 = (f32[3,16,16,128]{3,2,1,0:T(8,128)S(1)}, f32[3,16,16,128]{3,2,1,0:T(8,128)}, u32[]{:S(2)}) copy-start(f32[3,16,16,128]{3,2,1,0:T(8,128)} %param.9) | copy-start | bytes 1179652
  219.4 21.7 %copy-start.13 = (f32[16,16]{1,0:T(8,128)S(1)}, f32[16,16]{1,0:T(8,128)}, u32[]{:S(2)}) copy-start(f32[16,16]{1,0:T(8,128)} %param.10) | copy-start | bytes 3076
  220.4 26.8 %copy-start.11 = (s32[1024]{0:T(1024)S(1)}, s32[1024]{0:T(1024)}, u32[]{:S(2)}) copy-start(s32[1024]{0:T(1024)} %copy-done.10) | copy-start | bytes 12292
  222.1 26.0 %copy-start.15 = (pred[4,64]{1,0:T(4,128)(4,1)S(1)}, pred[4,64]{1,0:T(4,128)(4,1)}, u32[]{:S(2)}) copy-start(pred[4,64]{1,0:T(4,128)(4,1)} %copy-done.14) | copy-start | bytes 772
  224.5 208.3 %copy-start.8 = (pred[4096]{0:T(1024)(128)(4,1)S(1)}, pred[4096]{0:T(1024)(128)(4,1)}, u32[]{:S(2)}) copy-start(pred[4096]{0:T(1024)(128)(4,1)} %copy-done.7) | copy-start | bytes 12292
  225.7 4.3 collective-permute-start.8
  227.6 5.1 %collective-permute-start.9 = (f32[3,1,16,128]{3,2,1,0:T(8,128)S(1)}, f32[3,1,16,128]{3,2,1,0:T(8,128)S(1)}, u32[]{:S(2)}, u32[]{:S(2)}) collective-permute-start(f32[3,1,16,128]{3,2,1,0:T(8,128)S(1)} %get-tuple-element.17), channel_id=1, source_target_pairs={{0,16},{16,32},{32,48},{48,64},{64,80},{80,96},{96,112},{112,128},... | collective-permute-start | bytes 73736 | tf_op jit(solution)/shard_map/ppermute | solution.py:12
  232.8 8.2 %collective-permute-start.10 = (f32[3,18,1,128]{3,2,1,0:T(1,128)S(1)}, f32[3,18,1,128]{3,2,1,0:T(1,128)S(1)}, u32[]{:S(2)}, u32[]{:S(2)}) collective-permute-start(f32[3,18,1,128]{3,2,1,0:T(1,128)S(1)} %get-tuple-element.13), channel_id=1, source_target_pairs={{1,0},{2,1},{3,2},{4,3},{5,4},{6,5},{7,6},{8,7},{9,8},{10,9},{11,1... | collective-permute-start | bytes 82952 | tf_op jit(solution)/shard_map/ppermute | solution.py:15
  239.1 7.9 %collective-permute-start.11 = (f32[3,18,1,128]{3,2,1,0:T(1,128)S(1)}, f32[3,18,1,128]{3,2,1,0:T(1,128)S(1)}, u32[]{:S(2)}, u32[]{:S(2)}) collective-permute-start(f32[3,18,1,128]{3,2,1,0:T(1,128)S(1)} %get-tuple-element.14), channel_id=1, source_target_pairs={{0,1},{1,2},{2,3},{3,4},{4,5},{5,6},{6,7},{7,8},{8,9},{9,10},{10,1... | collective-permute-start | bytes 82952 | tf_op jit(solution)/shard_map/ppermute | solution.py:12
  248.2 13.6 %collective-permute-start.12 = (bf16[1,64,128]{2,1,0:T(8,128)(2,1)S(1)}, bf16[1,64,128]{2,1,0:T(8,128)(2,1)S(1)}, u32[]{:S(2)}, u32[]{:S(2)}) collective-permute-start(bf16[1,64,128]{2,1,0:T(8,128)(2,1)S(1)} %get-tuple-element.22), channel_id=1, source_target_pairs={{0,16},{16,32},{32,48},{48,64},{64,80},{80,96},{96,112},{112,128},... | collective-permute-start | bytes 49160 | tf_op jit(solution)/shard_map/ppermute | solution.py:12
  250.1 11.6 %collective-permute-start.13 = (bf16[1,64,128]{2,1,0:T(8,128)(2,1)S(1)}, bf16[1,64,128]{2,1,0:T(8,128)(2,1)S(1)}, u32[]{:S(2)}, u32[]{:S(2)}) collective-permute-start(bf16[1,64,128]{2,1,0:T(8,128)(2,1)S(1)} %get-tuple-element.21), channel_id=1, source_target_pairs={{16,0},{32,16},{48,32},{64,48},{80,64},{96,80},{112,96},{128,112},... | collective-permute-start | bytes 49160 | tf_op jit(solution)/shard_map/ppermute | solution.py:15
  253.8 8.0 %collective-permute-start.14 = (bf16[1,64,128]{2,1,0:T(8,128)(2,1)S(1)}, bf16[1,64,128]{2,1,0:T(8,128)(2,1)S(1)}, u32[]{:S(2)}, u32[]{:S(2)}) collective-permute-start(bf16[1,64,128]{2,1,0:T(8,128)(2,1)S(1)} %get-tuple-element.20), channel_id=1, source_target_pairs={{0,1},{1,2},{2,3},{3,4},{4,5},{5,6},{6,7},{7,8},{8,9},{9,10},{10,1... | collective-permute-start | bytes 49160 | tf_op jit(solution)/shard_map/ppermute | solution.py:12
  255.7 7.5 %collective-permute-start.15 = (bf16[1,64,128]{2,1,0:T(8,128)(2,1)S(1)}, bf16[1,64,128]{2,1,0:T(8,128)(2,1)S(1)}, u32[]{:S(2)}, u32[]{:S(2)}) collective-permute-start(bf16[1,64,128]{2,1,0:T(8,128)(2,1)S(1)} %get-tuple-element.19), channel_id=1, source_target_pairs={{1,0},{2,1},{3,2},{4,3},{5,4},{6,5},{7,6},{8,7},{9,8},{10,9},{11,1... | collective-permute-start | bytes 49160 | tf_op jit(solution)/shard_map/ppermute | solution.py:15
  263.2 0.7 copy-start.3
  436.3 20.4 %copy-start.19 = (s32[64]{0:T(128)S(1)}, s32[64]{0:T(128)}, u32[]{:S(2)}) copy-start(s32[64]{0:T(128)} %get-tuple-element.29) | copy-start | bytes 772
  436.3 21.5 %copy-start.18 = (s32[64]{0:T(128)S(1)}, s32[64]{0:T(128)}, u32[]{:S(2)}) copy-start(s32[64]{0:T(128)} %get-tuple-element.28) | copy-start | bytes 772
  436.4 22.6 %copy-start.17 = (s32[64]{0:T(128)S(1)}, s32[64]{0:T(128)}, u32[]{:S(2)}) copy-start(s32[64]{0:T(128)} %get-tuple-element.30) | copy-start | bytes 772
  436.4 23.6 %copy-start.16 = (s32[64]{0:T(128)S(1)}, s32[64]{0:T(128)}, u32[]{:S(2)}) copy-start(s32[64]{0:T(128)} %get-tuple-element.27) | copy-start | bytes 772
  437.1 15.5 %collective-permute-start.16 = (f32[1,64,128]{1,2,0:T(8,128)}, f32[1,64,128]{1,2,0:T(8,128)S(1)}, u32[]{:S(2)}, u32[]{:S(2)}) collective-permute-start(f32[1,64,128]{1,2,0:T(8,128)} %get-tuple-element.6), channel_id=1, source_target_pairs={{0,16},{16,32},{32,48},{48,64},{64,80},{80,96},{96,112},{112,128},... | collective-permute-start | bytes 98312 | tf_op jit(solution)/shard_map/ppermute | solution.py:12
  439.3 14.9 %collective-permute-start.17 = (f32[1,64,128]{1,2,0:T(8,128)}, f32[1,64,128]{1,2,0:T(8,128)}, u32[]{:S(2)}, u32[]{:S(2)}) collective-permute-start(f32[1,64,128]{1,2,0:T(8,128)} %get-tuple-element.5), channel_id=1, source_target_pairs={{16,0},{32,16},{48,32},{64,48},{80,64},{96,80},{112,96},{128,112},... | collective-permute-start | bytes 98312 | tf_op jit(solution)/shard_map/ppermute | solution.py:15
  442.7 12.4 %collective-permute-start.18 = (f32[1,64,128]{1,2,0:T(8,128)}, f32[1,64,128]{1,2,0:T(8,128)S(1)}, u32[]{:S(2)}, u32[]{:S(2)}) collective-permute-start(f32[1,64,128]{1,2,0:T(8,128)} %get-tuple-element.4), channel_id=1, source_target_pairs={{0,1},{1,2},{2,3},{3,4},{4,5},{5,6},{6,7},{7,8},{8,9},{9,10},{10,1... | collective-permute-start | bytes 98312 | tf_op jit(solution)/shard_map/ppermute | solution.py:12
  446.0 10.7 %collective-permute-start.19 = (f32[1,64,128]{1,2,0:T(8,128)}, f32[1,64,128]{1,2,0:T(8,128)S(1)}, u32[]{:S(2)}, u32[]{:S(2)}) collective-permute-start(f32[1,64,128]{1,2,0:T(8,128)} %get-tuple-element.3), channel_id=1, source_target_pairs={{1,0},{2,1},{3,2},{4,3},{5,4},{6,5},{7,6},{8,7},{9,8},{10,9},{11,1... | collective-permute-start | bytes 98312 | tf_op jit(solution)/shard_map/ppermute | solution.py:15
  452.6 0.6 copy-start.6
  455.1 0.6 copy-start.5
  461.2 18.4 %copy-start.2 = (f32[3,16,16,128]{3,2,1,0:T(8,128)}, f32[3,16,16,128]{3,2,1,0:T(8,128)S(1)}, u32[]{:S(2)}) copy-start(f32[3,16,16,128]{3,2,1,0:T(8,128)S(1)} %add.126) | copy-start | bytes 1179652
  461.2 4.3 collective-permute-start.20
  463.1 5.1 %collective-permute-start.21 = (f32[3,1,16,128]{3,2,1,0:T(8,128)S(1)}, f32[3,1,16,128]{3,2,1,0:T(8,128)S(1)}, u32[]{:S(2)}, u32[]{:S(2)}) collective-permute-start(f32[3,1,16,128]{3,2,1,0:T(8,128)S(1)} %get-tuple-element.15), channel_id=1, source_target_pairs={{0,16},{16,32},{32,48},{48,64},{64,80},{80,96},{96,112},{112,128},... | collective-permute-start | bytes 73736 | tf_op jit(solution)/shard_map/ppermute | solution.py:12
  468.3 5.9 %collective-permute-start.22 = (f32[3,18,1,128]{3,2,1,0:T(1,128)S(1)}, f32[3,18,1,128]{3,2,1,0:T(1,128)S(1)}, u32[]{:S(2)}, u32[]{:S(2)}) collective-permute-start(f32[3,18,1,128]{3,2,1,0:T(1,128)S(1)} %get-tuple-element.11), channel_id=1, source_target_pairs={{1,0},{2,1},{3,2},{4,3},{5,4},{6,5},{7,6},{8,7},{9,8},{10,9},{11,1... | collective-permute-start | bytes 82952 | tf_op jit(solution)/shard_map/ppermute | solution.py:15
  470.8 7.9 %collective-permute-start.23 = (f32[3,18,1,128]{3,2,1,0:T(1,128)S(1)}, f32[3,18,1,128]{3,2,1,0:T(1,128)S(1)}, u32[]{:S(2)}, u32[]{:S(2)}) collective-permute-start(f32[3,18,1,128]{3,2,1,0:T(1,128)S(1)} %get-tuple-element.12), channel_id=1, source_target_pairs={{0,1},{1,2},{2,3},{3,4},{4,5},{5,6},{6,7},{7,8},{8,9},{9,10},{10,1... | collective-permute-start | bytes 82952 | tf_op jit(solution)/shard_map/ppermute | solution.py:12
Sparse Core Ops, SparseCore 0:
  28.0 173.6 all-gather.2
  264.8 168.0 all-gather.4
where the time goes:
time: 488 us; the launch traced here: 486 us
  waiting for transfers between devices  349 us (72%)
  starting transfers between devices  76.8 us (16%)
  local copies, waits for them, and re-layouts  22.8 us (5%)
  between operations  14.8 us (3%)
  other arithmetic  14.4 us (3%)
  matrix products  8.25 us (2%)
    all_gather x2, waiting for transfers between devices, coarse_solve(): lax.all_gather(coarse_in, ('gx', 'gy'), axis=0, tiled=True)  331 us
    ppermute x12, starting transfers between devices, with_halo(): lax.ppermute(lax.slice_in_dim(block, 0, width, axis=dim), axis, backward)  46.6 us
    ppermute x12, starting transfers between devices, with_halo(): lax.ppermute(lax.slice_in_dim(block, block.shape[dim] - width, None, axis...  30.1 us
    ppermute x12, waiting for transfers between devices, with_halo(): lax.ppermute(lax.slice_in_dim(block, block.shape[dim] - width, None, axis...  15.9 us
  transfers between devices with their start and end apart: 26, of which 9 were waited for; matrix products, arithmetic and copies ran while one was open for 4% of the time, Pallas kernels for 0%

commit v1 on v0

--- a/solution.py
+++ b/solution.py
@@ -34,7 +34,12 @@
 def coarse_solve(coarse_in, ordered):
     return jnp.dot(
         ordered,
-        lax.all_gather(coarse_in, ("gx", "gy"), axis=0, tiled=True),
+        jnp.concatenate(
+            lax.all_to_all(
+                jnp.stack([coarse_in] * lax.axis_size(("gx", "gy"))), ("gx", "gy"), 0, 0
+            ),
+            axis=0,
+        ),
         preferred_element_type=jnp.float32,
     )
 

time: 488 us -> 283 us (0.58)
  the two profiles are of different devices: /device:TPU:40 before, /device:TPU:9 now
where the time goes in v1:
time: 283 us; the launch traced here: 281 us
  starting transfers between devices  100 us (35%)
  blocking collectives  69 us (24%)
  waiting for transfers between devices  67.7 us (24%)
  local copies, waits for them, and re-layouts  16.4 us (6%)
  other arithmetic  13.8 us (5%)
  matrix products  12.6 us (4%)
    all_to_all x1, blocking collectives, coarse_solve(): lax.all_to_all(jnp.stack([coarse_in] * lax.axis_size(('gx', 'gy'))), ('gx...  69 us
    all_to_all x1, waiting for transfers between devices, coarse_solve(): lax.all_to_all(jnp.stack([coarse_in] * lax.axis_size(('gx', 'gy'))), ('gx...  48 us
    ppermute x12, starting transfers between devices, with_halo(): lax.ppermute(lax.slice_in_dim(block, 0, width, axis=dim), axis, backward)  40.3 us
    ppermute x12, starting transfers between devices, with_halo(): lax.ppermute(lax.slice_in_dim(block, block.shape[dim] - width, None, axis...  32.2 us
    all_to_all x1, starting transfers between devices, coarse_solve(): lax.all_to_all(jnp.stack([coarse_in] * lax.axis_size(('gx', 'gy'))), ('gx...  28 us
    ppermute x12, waiting for transfers between devices, with_halo(): lax.ppermute(lax.slice_in_dim(block, block.shape[dim] - width, None, axis...  10.1 us
    ppermute x12, waiting for transfers between devices, with_halo(): lax.ppermute(lax.slice_in_dim(block, 0, width, axis=dim), axis, backward)  9.57 us
    dot_general x2, matrix products, precondition(): lax.dot_general(basis_rows, coarse_out, (((0,), (0,)), ((), ())), preferr...  8.62 us
  transfers between devices with their start and end apart: 25, of which 7 were waited for; matrix products, arithmetic and copies ran while one was open for 4% of the time, Pallas kernels for 0%

profile of v1, /device:TPU:9, one launch (start us, length us, event | category | flops | bytes accessed | tf_op | source)
XLA Modules:
  0.0 281.4 jit_solution(17233942499902118376)
XLA Ops:
  2.3 1.7 gather_fusion.1
  4.1 4.3 %collective-permute-start.3 = (bf16[1,64,128]{2,1,0:T(8,128)(2,1)S(1)}, bf16[1,64,128]{2,1,0:T(8,128)(2,1)S(1)}, u32[]{:S(2)}, u32[]{:S(2)}) collective-permute-start(bf16[1,64,128]{2,1,0:T(8,128)(2,1)S(1)} %get-tuple-element.23), channel_id=1, source_target_pairs={{1,0},{2,1},{3,2},{4,3},{5,4},{6,5},{7,6},{8,7},{9,8},{10,9},{11,1... | collective-permute-start | bytes 49160 | tf_op jit(solution)/shard_map/ppermute | solution.py:15
  8.4 1.9 collective-permute-start.2
  10.3 2.9 %collective-permute-start.1 = (bf16[1,64,128]{2,1,0:T(8,128)(2,1)S(1)}, bf16[1,64,128]{2,1,0:T(8,128)(2,1)S(1)}, u32[]{:S(2)}, u32[]{:S(2)}) collective-permute-start(bf16[1,64,128]{2,1,0:T(8,128)(2,1)S(1)} %get-tuple-element.25), channel_id=1, source_target_pairs={{16,0},{32,16},{48,32},{64,48},{80,64},{96,80},{112,96},{128,112},... | collective-permute-start | bytes 49160 | tf_op jit(solution)/shard_map/ppermute | solution.py:15
  13.2 3.6 %collective-permute-start = (bf16[1,64,128]{2,1,0:T(8,128)(2,1)S(1)}, bf16[1,64,128]{2,1,0:T(8,128)(2,1)S(1)}, u32[]{:S(2)}, u32[]{:S(2)}) collective-permute-start(bf16[1,64,128]{2,1,0:T(8,128)(2,1)S(1)} %get-tuple-element.26), channel_id=1, source_target_pairs={{0,16},{16,32},{32,48},{48,64},{64,80},{80,96},{96,112},{112,128},... | collective-permute-start | bytes 49160 | tf_op jit(solution)/shard_map/ppermute | solution.py:12
  19.0 1.2 stack.20
  20.1 28.0 %all-to-all-start = ((bf16[512,8,128]{2,1,0:T(8,128)(2,1)}), bf16[512,8,128]{2,1,0:T(8,128)(2,1)}, u32[]{:S(2)}, u32[]{:S(2)}) async-start(bf16[512,8,128]{2,1,0:T(8,128)(2,1)} %stack.20), calls=%async_computation | async-start | bytes 2097152 | tf_op jit(solution)/shard_map/all_to_all | solution.py:38
  48.1 2.2 reshape_squeeze.3
  50.3 1.9 copy.19
  52.3 2.4 gather_fusion
  54.7 48.0 %all-to-all-done = bf16[512,8,128]{2,1,0:T(8,128)(2,1)} async-done(((bf16[512,8,128]{2,1,0:T(8,128)(2,1)}), bf16[512,8,128]{2,1,0:T(8,128)(2,1)}, u32[]{:S(2)}, u32[]{:S(2)}) %all-to-all-start) | async-done | bytes 1048608 | tf_op jit(solution)/shard_map/all_to_all | solution.py:38
  102.7 3.9 %fusion.21 = f32[128,1024]{1,0:T(8,128)S(1)} fusion(bf16[512,8,128]{2,1,0:T(8,128)(2,1)} %all-to-all-done, bf16[512,8,8]{2,1,0:T(8,128)(2,1)} %gather_fusion, pred[512]{0:T(512)(128)(4,1)S(1)} %compare_and_fusion.1, bf16[1,1,8,1024]{3,2,1,0:T(8,128)(2,1)S(1)} %copy-done.4), kind=kOutput, calls=%fused_computation.28 | convolution fusion | flops 10519552 | bytes 1655296 | tf_op jit(solution)/shard_map/dot_general | solution.py:61
  108.3 3.9 %collective-permute-start.7 = (f32[1,64,128]{1,2,0:T(8,128)}, f32[1,64,128]{1,2,0:T(8,128)S(1)}, u32[]{:S(2)}, u32[]{:S(2)}) collective-permute-start(f32[1,64,128]{1,2,0:T(8,128)} %get-tuple-element.7), channel_id=1, source_target_pairs={{1,0},{2,1},{3,2},{4,3},{5,4},{6,5},{7,6},{8,7},{9,8},{10,9},{11,1... | collective-permute-start | bytes 98312 | tf_op jit(solution)/shard_map/ppermute | solution.py:15
  112.2 1.9 collective-permute-start.6
  114.1 3.1 %collective-permute-start.5 = (f32[1,64,128]{1,2,0:T(8,128)}, f32[1,64,128]{1,2,0:T(8,128)S(1)}, u32[]{:S(2)}, u32[]{:S(2)}) collective-permute-start(f32[1,64,128]{1,2,0:T(8,128)} %get-tuple-element.9), channel_id=1, source_target_pairs={{16,0},{32,16},{48,32},{64,48},{80,64},{96,80},{112,96},{128,112},... | collective-permute-start | bytes 98312 | tf_op jit(solution)/shard_map/ppermute | solution.py:15
  117.2 2.9 %collective-permute-start.4 = (f32[1,64,128]{1,2,0:T(8,128)}, f32[1,64,128]{1,2,0:T(8,128)S(1)}, u32[]{:S(2)}, u32[]{:S(2)}) collective-permute-start(f32[1,64,128]{1,2,0:T(8,128)} %get-tuple-element.10), channel_id=1, source_target_pairs={{0,16},{16,32},{32,48},{48,64},{64,80},{80,96},{96,112},{112,128},... | collective-permute-start | bytes 98312 | tf_op jit(solution)/shard_map/ppermute | solution.py:12
  121.8 1.2 scatter_fusion
  123.0 1.2 scatter_fusion.1
  124.2 1.1 scatter_fusion.2
  125.3 1.1 scatter_fusion.3
  126.4 4.2 %collective-permute-start.9 = (f32[3,1,16,128]{3,2,1,0:T(8,128)S(1)}, f32[3,1,16,128]{3,2,1,0:T(8,128)S(1)}, u32[]{:S(2)}, u32[]{:S(2)}) collective-permute-start(f32[3,1,16,128]{3,2,1,0:T(8,128)S(1)} %get-tuple-element.17), channel_id=1, source_target_pairs={{0,16},{16,32},{32,48},{48,64},{64,80},{80,96},{96,112},{112,128},... | collective-permute-start | bytes 73736 | tf_op jit(solution)/shard_map/ppermute | solution.py:12
  130.6 1.9 collective-permute-start.8
  132.5 3.2 %collective-permute-done.8 = f32[3,1,16,128]{3,2,1,0:T(8,128)S(1)} collective-permute-done((f32[3,1,16,128]{3,2,1,0:T(8,128)S(1)}, f32[3,1,16,128]{3,2,1,0:T(8,128)S(1)}, u32[]{:S(2)}, u32[]{:S(2)}) %collective-permute-start.8) | collective-permute-done | bytes 24608 | tf_op jit(solution)/shard_map/ppermute | solution.py:15
  135.8 5.8 %collective-permute-start.10 = (f32[3,18,1,128]{3,2,1,0:T(1,128)S(1)}, f32[3,18,1,128]{3,2,1,0:T(1,128)S(1)}, u32[]{:S(2)}, u32[]{:S(2)}) collective-permute-start(f32[3,18,1,128]{3,2,1,0:T(1,128)S(1)} %get-tuple-element.13), channel_id=1, source_target_pairs={{1,0},{2,1},{3,2},{4,3},{5,4},{6,5},{7,6},{8,7},{9,8},{10,9},{11,1... | collective-permute-start | bytes 82952 | tf_op jit(solution)/shard_map/ppermute | solution.py:15
  141.5 1.9 collective-permute-start.11
  143.5 4.8 %collective-permute-done.11 = f32[3,18,1,128]{3,2,1,0:T(1,128)S(1)} collective-permute-done((f32[3,18,1,128]{3,2,1,0:T(1,128)S(1)}, f32[3,18,1,128]{3,2,1,0:T(1,128)S(1)}, u32[]{:S(2)}, u32[]{:S(2)}) %collective-permute-start.11) | collective-permute-done | bytes 27680 | tf_op jit(solution)/shard_map/ppermute | solution.py:12
  149.4 3.4 %collective-permute-start.12 = (bf16[1,64,128]{2,1,0:T(8,128)(2,1)S(1)}, bf16[1,64,128]{2,1,0:T(8,128)(2,1)S(1)}, u32[]{:S(2)}, u32[]{:S(2)}) collective-permute-start(bf16[1,64,128]{2,1,0:T(8,128)(2,1)S(1)} %get-tuple-element.22), channel_id=1, source_target_pairs={{0,16},{16,32},{32,48},{48,64},{64,80},{80,96},{96,112},{112,128},... | collective-permute-start | bytes 49160 | tf_op jit(solution)/shard_map/ppermute | solution.py:12
  152.8 1.9 collective-permute-start.15
  154.7 3.4 %collective-permute-start.14 = (bf16[1,64,128]{2,1,0:T(8,128)(2,1)S(1)}, bf16[1,64,128]{2,1,0:T(8,128)(2,1)S(1)}, u32[]{:S(2)}, u32[]{:S(2)}) collective-permute-start(bf16[1,64,128]{2,1,0:T(8,128)(2,1)S(1)} %get-tuple-element.20), channel_id=1, source_target_pairs={{0,1},{1,2},{2,3},{3,4},{4,5},{5,6},{6,7},{7,8},{8,9},{9,10},{10,1... | collective-permute-start | bytes 49160 | tf_op jit(solution)/shard_map/ppermute | solution.py:12
  158.1 1.9 collective-permute-start.13
  160.1 3.1 %collective-permute-done.13 = bf16[1,64,128]{2,1,0:T(8,128)(2,1)S(1)} collective-permute-done((bf16[1,64,128]{2,1,0:T(8,128)(2,1)S(1)}, bf16[1,64,128]{2,1,0:T(8,128)(2,1)S(1)}, u32[]{:S(2)}, u32[]{:S(2)}) %collective-permute-start.13) | collective-permute-done | bytes 16416 | tf_op jit(solution)/shard_map/ppermute | solution.py:15
  163.7 69.0 %all_to_all.10 = bf16[512,8,128]{2,1,0:T(8,128)(2,1)} all-to-all(bf16[512,8,128]{2,1,0:T(8,128)(2,1)S(1)} %stack.25), channel_id=1, replica_groups=mesh['gx'=32,'gy'=16] {'gx','gy'}, dimensions={0} | all-to-all | bytes 2097152 | tf_op jit(solution)/shard_map/all_to_all | solution.py:38
  232.8 4.7 %fusion.20 = f32[128,1024]{1,0:T(8,128)} fusion(bf16[512,8,128]{2,1,0:T(8,128)(2,1)} %all_to_all.10, bf16[512,8,8]{2,1,0:T(8,128)(2,1)} %gather_fusion, pred[512]{0:T(512)(128)(4,1)S(1)} %copy-done.15, bf16[1,1,8,1024]{3,2,1,0:T(8,128)(2,1)S(1)} %copy-done.5), kind=kOutput, calls=%fused_computation.27 | convolution fusion | flops 10519552 | bytes 1655296 | tf_op jit(solution)/shard_map/dot_general | solution.py:61
  237.5 1.9 fusion.13
  240.1 3.9 %collective-permute-start.19 = (f32[1,64,128]{1,2,0:T(8,128)}, f32[1,64,128]{1,2,0:T(8,128)S(1)}, u32[]{:S(2)}, u32[]{:S(2)}) collective-permute-start(f32[1,64,128]{1,2,0:T(8,128)} %get-tuple-element.3), channel_id=1, source_target_pairs={{1,0},{2,1},{3,2},{4,3},{5,4},{6,5},{7,6},{8,7},{9,8},{10,9},{11,1... | collective-permute-start | bytes 98312 | tf_op jit(solution)/shard_map/ppermute | solution.py:15
  244.1 1.9 collective-permute-start.18
  246.0 3.1 %collective-permute-start.17 = (f32[1,64,128]{1,2,0:T(8,128)}, f32[1,64,128]{1,2,0:T(8,128)S(1)}, u32[]{:S(2)}, u32[]{:S(2)}) collective-permute-start(f32[1,64,128]{1,2,0:T(8,128)} %get-tuple-element.5), channel_id=1, source_target_pairs={{16,0},{32,16},{48,32},{64,48},{80,64},{96,80},{112,96},{128,112},... | collective-permute-start | bytes 98312 | tf_op jit(solution)/shard_map/ppermute | solution.py:15
  249.1 2.9 %collective-permute-start.16 = (f32[1,64,128]{1,2,0:T(8,128)}, f32[1,64,128]{1,2,0:T(8,128)S(1)}, u32[]{:S(2)}, u32[]{:S(2)}) collective-permute-start(f32[1,64,128]{1,2,0:T(8,128)} %get-tuple-element.6), channel_id=1, source_target_pairs={{0,16},{16,32},{32,48},{48,64},{64,80},{80,96},{96,112},{112,128},... | collective-permute-start | bytes 98312 | tf_op jit(solution)/shard_map/ppermute | solution.py:12
  252.7 1.1 copy.27
  255.7 1.2 scatter_fusion.4
  256.9 1.2 scatter_fusion.5
  258.1 1.1 scatter_fusion.6
  260.4 2.4 collective-permute-start.21
  262.8 1.9 collective-permute-start.20
  264.7 3.2 %collective-permute-done.20 = f32[3,1,16,128]{3,2,1,0:T(8,128)S(1)} collective-permute-done((f32[3,1,16,128]{3,2,1,0:T(8,128)S(1)}, f32[3,1,16,128]{3,2,1,0:T(8,128)S(1)}, u32[]{:S(2)}, u32[]{:S(2)}) %collective-permute-start.20) | collective-permute-done | bytes 24608 | tf_op jit(solution)/shard_map/ppermute | solution.py:15
  268.0 5.8 %collective-permute-start.22 = (f32[3,18,1,128]{3,2,1,0:T(1,128)S(1)}, f32[3,18,1,128]{3,2,1,0:T(1,128)S(1)}, u32[]{:S(2)}, u32[]{:S(2)}) collective-permute-start(f32[3,18,1,128]{3,2,1,0:T(1,128)S(1)} %get-tuple-element.11), channel_id=1, source_target_pairs={{1,0},{2,1},{3,2},{4,3},{5,4},{6,5},{7,6},{8,7},{9,8},{10,9},{11,1... | collective-permute-start | bytes 82952 | tf_op jit(solution)/shard_map/ppermute | solution.py:15
  273.7 1.9 collective-permute-start.23
  275.7 4.8 %collective-permute-done.23 = f32[3,18,1,128]{3,2,1,0:T(1,128)S(1)} collective-permute-done((f32[3,18,1,128]{3,2,1,0:T(1,128)S(1)}, f32[3,18,1,128]{3,2,1,0:T(1,128)S(1)}, u32[]{:S(2)}, u32[]{:S(2)}) %collective-permute-start.23) | collective-permute-done | bytes 27680 | tf_op jit(solution)/shard_map/ppermute | solution.py:12
  (102 shorter events, 14.3 us)
Async XLA Ops:
  0.6 106.0 %copy-start = (bf16[1,1,1024,1024]{3,2,1,0:T(8,128)(2,1)S(1)}, bf16[1,1,1024,1024]{3,2,1,0:T(8,128)(2,1)}, u32[]{:S(2)}) copy-start(bf16[1,1,1024,1024]{3,2,1,0:T(8,128)(2,1)} %param.11) | copy-start | bytes 6291460
  4.1 13.8 %collective-permute-start.3 = (bf16[1,64,128]{2,1,0:T(8,128)(2,1)S(1)}, bf16[1,64,128]{2,1,0:T(8,128)(2,1)S(1)}, u32[]{:S(2)}, u32[]{:S(2)}) collective-permute-start(bf16[1,64,128]{2,1,0:T(8,128)(2,1)S(1)} %get-tuple-element.23), channel_id=1, source_target_pairs={{1,0},{2,1},{3,2},{4,3},{5,4},{6,5},{7,6},{8,7},{9,8},{10,9},{11,1... | collective-permute-start | bytes 49160 | tf_op jit(solution)/shard_map/ppermute | solution.py:15
  8.4 9.5 %collective-permute-start.2 = (bf16[1,64,128]{2,1,0:T(8,128)(2,1)S(1)}, bf16[1,64,128]{2,1,0:T(8,128)(2,1)S(1)}, u32[]{:S(2)}, u32[]{:S(2)}) collective-permute-start(bf16[1,64,128]{2,1,0:T(8,128)(2,1)S(1)} %get-tuple-element.24), channel_id=1, source_target_pairs={{0,1},{1,2},{2,3},{3,4},{4,5},{5,6},{6,7},{7,8},{8,9},{9,10},{10,1... | collective-permute-start | bytes 49160 | tf_op jit(solution)/shard_map/ppermute | solution.py:12
  10.3 7.5 %collective-permute-start.1 = (bf16[1,64,128]{2,1,0:T(8,128)(2,1)S(1)}, bf16[1,64,128]{2,1,0:T(8,128)(2,1)S(1)}, u32[]{:S(2)}, u32[]{:S(2)}) collective-permute-start(bf16[1,64,128]{2,1,0:T(8,128)(2,1)S(1)} %get-tuple-element.25), channel_id=1, source_target_pairs={{16,0},{32,16},{48,32},{64,48},{80,64},{96,80},{112,96},{128,112},... | collective-permute-start | bytes 49160 | tf_op jit(solution)/shard_map/ppermute | solution.py:15
  13.2 34.9 %copy-start.3 = (bf16[1,1,8,4096]{3,2,1,0:T(8,128)(2,1)S(1)}, bf16[1,1,8,4096]{3,2,1,0:T(8,128)(2,1)}, u32[]{:S(2)}) copy-start(bf16[1,1,8,4096]{3,2,1,0:T(8,128)(2,1)} %param.13) | copy-start | bytes 196612
  13.2 4.6 %collective-permute-start = (bf16[1,64,128]{2,1,0:T(8,128)(2,1)S(1)}, bf16[1,64,128]{2,1,0:T(8,128)(2,1)S(1)}, u32[]{:S(2)}, u32[]{:S(2)}) collective-permute-start(bf16[1,64,128]{2,1,0:T(8,128)(2,1)S(1)} %get-tuple-element.26), channel_id=1, source_target_pairs={{0,16},{16,32},{32,48},{48,64},{64,80},{80,96},{96,112},{112,128},... | collective-permute-start | bytes 49160 | tf_op jit(solution)/shard_map/ppermute | solution.py:12
  20.1 82.6 %all-to-all-start = ((bf16[512,8,128]{2,1,0:T(8,128)(2,1)}), bf16[512,8,128]{2,1,0:T(8,128)(2,1)}, u32[]{:S(2)}, u32[]{:S(2)}) async-start(bf16[512,8,128]{2,1,0:T(8,128)(2,1)} %stack.20), calls=%async_computation | async-start | bytes 2097152 | tf_op jit(solution)/shard_map/all_to_all | solution.py:38
  48.1 4.2 %copy-start.8 = (s32[512]{0:T(512)S(1)}, s32[512]{0:T(512)}, u32[]{:S(2)}) copy-start(s32[512]{0:T(512)} %param.15) | copy-start | bytes 6148
  50.3 52.4 %copy-start.4 = (bf16[1,1,8,1024]{3,2,1,0:T(8,128)(2,1)S(1)}, bf16[1,1,8,1024]{3,2,1,0:T(8,128)(2,1)}, u32[]{:S(2)}) copy-start(bf16[1,1,8,1024]{3,2,1,0:T(8,128)(2,1)} %param.12) | copy-start | bytes 49156
  54.7 52.8 %copy-start.14 = (pred[512]{0:T(512)(128)(4,1)}, pred[512]{0:T(512)(128)(4,1)S(1)}, u32[]{:S(2)}) copy-start(pred[512]{0:T(512)(128)(4,1)S(1)} %compare_and_fusion.1) | copy-start | bytes 1540
  106.7 13.4 %copy-start.7 = (s32[1,1,4,64]{3,2,1,0:T(4,128)S(1)}, s32[1,1,4,64]{3,2,1,0:T(4,128)}, u32[]{:S(2)}) copy-start(s32[1,1,4,64]{3,2,1,0:T(4,128)} %param.14) | copy-start | bytes 3076
  108.3 12.6 %collective-permute-start.7 = (f32[1,64,128]{1,2,0:T(8,128)}, f32[1,64,128]{1,2,0:T(8,128)S(1)}, u32[]{:S(2)}, u32[]{:S(2)}) collective-permute-start(f32[1,64,128]{1,2,0:T(8,128)} %get-tuple-element.7), channel_id=1, source_target_pairs={{1,0},{2,1},{3,2},{4,3},{5,4},{6,5},{7,6},{8,7},{9,8},{10,9},{11,1... | collective-permute-start | bytes 98312 | tf_op jit(solution)/shard_map/ppermute | solution.py:15
  112.2 8.8 %collective-permute-start.6 = (f32[1,64,128]{1,2,0:T(8,128)}, f32[1,64,128]{1,2,0:T(8,128)S(1)}, u32[]{:S(2)}, u32[]{:S(2)}) collective-permute-start(f32[1,64,128]{1,2,0:T(8,128)} %get-tuple-element.8), channel_id=1, source_target_pairs={{0,1},{1,2},{2,3},{3,4},{4,5},{5,6},{6,7},{7,8},{8,9},{9,10},{10,1... | collective-permute-start | bytes 98312 | tf_op jit(solution)/shard_map/ppermute | solution.py:12
  114.1 6.9 %collective-permute-start.5 = (f32[1,64,128]{1,2,0:T(8,128)}, f32[1,64,128]{1,2,0:T(8,128)S(1)}, u32[]{:S(2)}, u32[]{:S(2)}) collective-permute-start(f32[1,64,128]{1,2,0:T(8,128)} %get-tuple-element.9), channel_id=1, source_target_pairs={{16,0},{32,16},{48,32},{64,48},{80,64},{96,80},{112,96},{128,112},... | collective-permute-start | bytes 98312 | tf_op jit(solution)/shard_map/ppermute | solution.py:15
  117.2 4.5 %collective-permute-start.4 = (f32[1,64,128]{1,2,0:T(8,128)}, f32[1,64,128]{1,2,0:T(8,128)S(1)}, u32[]{:S(2)}, u32[]{:S(2)}) collective-permute-start(f32[1,64,128]{1,2,0:T(8,128)} %get-tuple-element.10), channel_id=1, source_target_pairs={{0,16},{16,32},{32,48},{48,64},{64,80},{80,96},{96,112},{112,128},... | collective-permute-start | bytes 98312 | tf_op jit(solution)/shard_map/ppermute | solution.py:12
  120.7 5.7 %copy-start.10 = (s32[64]{0:T(128)}, s32[64]{0:T(128)S(1)}, u32[]{:S(2)}) copy-start(s32[64]{0:T(128)S(1)} %get-tuple-element.27) | copy-start | bytes 772
  120.7 5.7 %copy-start.12 = (s32[64]{0:T(128)}, s32[64]{0:T(128)S(1)}, u32[]{:S(2)}) copy-start(s32[64]{0:T(128)S(1)} %get-tuple-element.30) | copy-start | bytes 772
  120.7 27.5 %copy-start.1 = (f32[3,16,16,128]{3,2,1,0:T(8,128)S(1)}, f32[3,16,16,128]{3,2,1,0:T(8,128)}, u32[]{:S(2)}) copy-start(f32[3,16,16,128]{3,2,1,0:T(8,128)} %param.9) | copy-start | bytes 1179652
  120.9 22.6 %copy-start.9 = (f32[16,16]{1,0:T(8,128)S(1)}, f32[16,16]{1,0:T(8,128)}, u32[]{:S(2)}) copy-start(f32[16,16]{1,0:T(8,128)} %param.10) | copy-start | bytes 3076
  124.2 39.0 %copy-start.5 = (bf16[1,1,8,1024]{3,2,1,0:T(8,128)(2,1)S(1)}, bf16[1,1,8,1024]{3,2,1,0:T(8,128)(2,1)}, u32[]{:S(2)}) copy-start(bf16[1,1,8,1024]{3,2,1,0:T(8,128)(2,1)} %param.12) | copy-start | bytes 49156
  126.4 6.1 %collective-permute-start.9 = (f32[3,1,16,128]{3,2,1,0:T(8,128)S(1)}, f32[3,1,16,128]{3,2,1,0:T(8,128)S(1)}, u32[]{:S(2)}, u32[]{:S(2)}) collective-permute-start(f32[3,1,16,128]{3,2,1,0:T(8,128)S(1)} %get-tuple-element.17), channel_id=1, source_target_pairs={{0,16},{16,32},{32,48},{48,64},{64,80},{80,96},{96,112},{112,128},... | collective-permute-start | bytes 73736 | tf_op jit(solution)/shard_map/ppermute | solution.py:12
  130.6 5.1 %collective-permute-start.8 = (f32[3,1,16,128]{3,2,1,0:T(8,128)S(1)}, f32[3,1,16,128]{3,2,1,0:T(8,128)S(1)}, u32[]{:S(2)}, u32[]{:S(2)}) collective-permute-start(f32[3,1,16,128]{3,2,1,0:T(8,128)S(1)} %get-tuple-element.18), channel_id=1, source_target_pairs={{16,0},{32,16},{48,32},{64,48},{80,64},{96,80},{112,96},{128,112},... | collective-permute-start | bytes 73736 | tf_op jit(solution)/shard_map/ppermute | solution.py:15
  135.8 7.7 %collective-permute-start.10 = (f32[3,18,1,128]{3,2,1,0:T(1,128)S(1)}, f32[3,18,1,128]{3,2,1,0:T(1,128)S(1)}, u32[]{:S(2)}, u32[]{:S(2)}) collective-permute-start(f32[3,18,1,128]{3,2,1,0:T(1,128)S(1)} %get-tuple-element.13), channel_id=1, source_target_pairs={{1,0},{2,1},{3,2},{4,3},{5,4},{6,5},{7,6},{8,7},{9,8},{10,9},{11,1... | collective-permute-start | bytes 82952 | tf_op jit(solution)/shard_map/ppermute | solution.py:15
  141.5 6.7 %collective-permute-start.11 = (f32[3,18,1,128]{3,2,1,0:T(1,128)S(1)}, f32[3,18,1,128]{3,2,1,0:T(1,128)S(1)}, u32[]{:S(2)}, u32[]{:S(2)}) collective-permute-start(f32[3,18,1,128]{3,2,1,0:T(1,128)S(1)} %get-tuple-element.14), channel_id=1, source_target_pairs={{0,1},{1,2},{2,3},{3,4},{4,5},{5,6},{6,7},{7,8},{8,9},{9,10},{10,1... | collective-permute-start | bytes 82952 | tf_op jit(solution)/shard_map/ppermute | solution.py:12
  149.4 83.4 %copy-start.15 = (pred[512]{0:T(512)(128)(4,1)S(1)}, pred[512]{0:T(512)(128)(4,1)}, u32[]{:S(2)}) copy-start(pred[512]{0:T(512)(128)(4,1)} %copy-done.14) | copy-start | bytes 1540
  149.4 10.6 %collective-permute-start.12 = (bf16[1,64,128]{2,1,0:T(8,128)(2,1)S(1)}, bf16[1,64,128]{2,1,0:T(8,128)(2,1)S(1)}, u32[]{:S(2)}, u32[]{:S(2)}) collective-permute-start(bf16[1,64,128]{2,1,0:T(8,128)(2,1)S(1)} %get-tuple-element.22), channel_id=1, source_target_pairs={{0,16},{16,32},{32,48},{48,64},{64,80},{80,96},{96,112},{112,128},... | collective-permute-start | bytes 49160 | tf_op jit(solution)/shard_map/ppermute | solution.py:12
  152.8 10.4 %collective-permute-start.15 = (bf16[1,64,128]{2,1,0:T(8,128)(2,1)S(1)}, bf16[1,64,128]{2,1,0:T(8,128)(2,1)S(1)}, u32[]{:S(2)}, u32[]{:S(2)}) collective-permute-start(bf16[1,64,128]{2,1,0:T(8,128)(2,1)S(1)} %get-tuple-element.19), channel_id=1, source_target_pairs={{1,0},{2,1},{3,2},{4,3},{5,4},{6,5},{7,6},{8,7},{9,8},{10,9},{11,1... | collective-permute-start | bytes 49160 | tf_op jit(solution)/shard_map/ppermute | solution.py:15
  154.7 8.4 %collective-permute-start.14 = (bf16[1,64,128]{2,1,0:T(8,128)(2,1)S(1)}, bf16[1,64,128]{2,1,0:T(8,128)(2,1)S(1)}, u32[]{:S(2)}, u32[]{:S(2)}) collective-permute-start(bf16[1,64,128]{2,1,0:T(8,128)(2,1)S(1)} %get-tuple-element.20), channel_id=1, source_target_pairs={{0,1},{1,2},{2,3},{3,4},{4,5},{5,6},{6,7},{7,8},{8,9},{9,10},{10,1... | collective-permute-start | bytes 49160 | tf_op jit(solution)/shard_map/ppermute | solution.py:12
  158.1 5.1 %collective-permute-start.13 = (bf16[1,64,128]{2,1,0:T(8,128)(2,1)S(1)}, bf16[1,64,128]{2,1,0:T(8,128)(2,1)S(1)}, u32[]{:S(2)}, u32[]{:S(2)}) collective-permute-start(bf16[1,64,128]{2,1,0:T(8,128)(2,1)S(1)} %get-tuple-element.21), channel_id=1, source_target_pairs={{16,0},{32,16},{48,32},{64,48},{80,64},{96,80},{112,96},{128,112},... | collective-permute-start | bytes 49160 | tf_op jit(solution)/shard_map/ppermute | solution.py:15
  239.4 18.7 %copy-start.13 = (s32[64]{0:T(128)S(1)}, s32[64]{0:T(128)}, u32[]{:S(2)}) copy-start(s32[64]{0:T(128)} %copy-done.12) | copy-start | bytes 772
  239.4 19.8 %copy-start.11 = (s32[64]{0:T(128)S(1)}, s32[64]{0:T(128)}, u32[]{:S(2)}) copy-start(s32[64]{0:T(128)} %copy-done.10) | copy-start | bytes 772
  240.1 13.7 %collective-permute-start.19 = (f32[1,64,128]{1,2,0:T(8,128)}, f32[1,64,128]{1,2,0:T(8,128)S(1)}, u32[]{:S(2)}, u32[]{:S(2)}) collective-permute-start(f32[1,64,128]{1,2,0:T(8,128)} %get-tuple-element.3), channel_id=1, source_target_pairs={{1,0},{2,1},{3,2},{4,3},{5,4},{6,5},{7,6},{8,7},{9,8},{10,9},{11,1... | collective-permute-start | bytes 98312 | tf_op jit(solution)/shard_map/ppermute | solution.py:15
  244.1 11.4 %collective-permute-start.18 = (f32[1,64,128]{1,2,0:T(8,128)}, f32[1,64,128]{1,2,0:T(8,128)S(1)}, u32[]{:S(2)}, u32[]{:S(2)}) collective-permute-start(f32[1,64,128]{1,2,0:T(8,128)} %get-tuple-element.4), channel_id=1, source_target_pairs={{0,1},{1,2},{2,3},{3,4},{4,5},{5,6},{6,7},{7,8},{8,9},{9,10},{10,1... | collective-permute-start | bytes 98312 | tf_op jit(solution)/shard_map/ppermute | solution.py:12
  246.0 9.5 %collective-permute-start.17 = (f32[1,64,128]{1,2,0:T(8,128)}, f32[1,64,128]{1,2,0:T(8,128)S(1)}, u32[]{:S(2)}, u32[]{:S(2)}) collective-permute-start(f32[1,64,128]{1,2,0:T(8,128)} %get-tuple-element.5), channel_id=1, source_target_pairs={{16,0},{32,16},{48,32},{64,48},{80,64},{96,80},{112,96},{128,112},... | collective-permute-start | bytes 98312 | tf_op jit(solution)/shard_map/ppermute | solution.py:15
  249.1 6.5 %collective-permute-start.16 = (f32[1,64,128]{1,2,0:T(8,128)}, f32[1,64,128]{1,2,0:T(8,128)S(1)}, u32[]{:S(2)}, u32[]{:S(2)}) collective-permute-start(f32[1,64,128]{1,2,0:T(8,128)} %get-tuple-element.6), channel_id=1, source_target_pairs={{0,16},{16,32},{32,48},{48,64},{64,80},{80,96},{96,112},{112,128},... | collective-permute-start | bytes 98312 | tf_op jit(solution)/shard_map/ppermute | solution.py:12
  253.9 0.6 copy-start.6
  260.4 21.0 %copy-start.2 = (f32[3,16,16,128]{3,2,1,0:T(8,128)}, f32[3,16,16,128]{3,2,1,0:T(8,128)S(1)}, u32[]{:S(2)}) copy-start(f32[3,16,16,128]{3,2,1,0:T(8,128)S(1)} %add.126) | copy-start | bytes 1179652
  260.4 4.3 %collective-permute-start.21 = (f32[3,1,16,128]{3,2,1,0:T(8,128)S(1)}, f32[3,1,16,128]{3,2,1,0:T(8,128)S(1)}, u32[]{:S(2)}, u32[]{:S(2)}) collective-permute-start(f32[3,1,16,128]{3,2,1,0:T(8,128)S(1)} %get-tuple-element.15), channel_id=1, source_target_pairs={{0,16},{16,32},{32,48},{48,64},{64,80},{80,96},{96,112},{112,128},... | collective-permute-start | bytes 73736 | tf_op jit(solution)/shard_map/ppermute | solution.py:12
  262.8 5.1 %collective-permute-start.20 = (f32[3,1,16,128]{3,2,1,0:T(8,128)S(1)}, f32[3,1,16,128]{3,2,1,0:T(8,128)S(1)}, u32[]{:S(2)}, u32[]{:S(2)}) collective-permute-start(f32[3,1,16,128]{3,2,1,0:T(8,128)S(1)} %get-tuple-element.16), channel_id=1, source_target_pairs={{16,0},{32,16},{48,32},{64,48},{80,64},{96,80},{112,96},{128,112},... | collective-permute-start | bytes 73736 | tf_op jit(solution)/shard_map/ppermute | solution.py:15
  268.0 7.7 %collective-permute-start.22 = (f32[3,18,1,128]{3,2,1,0:T(1,128)S(1)}, f32[3,18,1,128]{3,2,1,0:T(1,128)S(1)}, u32[]{:S(2)}, u32[]{:S(2)}) collective-permute-start(f32[3,18,1,128]{3,2,1,0:T(1,128)S(1)} %get-tuple-element.11), channel_id=1, source_target_pairs={{1,0},{2,1},{3,2},{4,3},{5,4},{6,5},{7,6},{8,7},{9,8},{10,9},{11,1... | collective-permute-start | bytes 82952 | tf_op jit(solution)/shard_map/ppermute | solution.py:15
  273.7 6.7 %collective-permute-start.23 = (f32[3,18,1,128]{3,2,1,0:T(1,128)S(1)}, f32[3,18,1,128]{3,2,1,0:T(1,128)S(1)}, u32[]{:S(2)}, u32[]{:S(2)}) collective-permute-start(f32[3,18,1,128]{3,2,1,0:T(1,128)S(1)} %get-tuple-element.12), channel_id=1, source_target_pairs={{0,1},{1,2},{2,3},{3,4},{4,5},{5,6},{6,7},{7,8},{8,9},{9,10},{10,1... | collective-permute-start | bytes 82952 | tf_op jit(solution)/shard_map/ppermute | solution.py:12
